TPU v7x, 32 devices: a whole 2x2x4 slice. The times are simulated.
32 devices in a mesh: groups: 2 (over x), node: 8 (over z, y), local: 2 (over core).
Axes of the slice: x: 2, y: 2, z: 4, core: 2. Of those that a mesh axis runs over, the one named last changes fastest.
Arguments:
- hidden_rows: bfloat16 [256, 7168], P(('groups', 'node', 'local')), parts along dimension 0, may hold values from -6 to 6
- expert_ids: int32 [256, 2], P(('groups', 'node', 'local')), parts along dimension 0, may hold values from 0 to 3, all different within a row; in each aligned block of 8 rows (0 to 7, 8 to 15, ...) at most 6 rows name the same one
- gate_values: float32 [256, 2], P(('groups', 'node', 'local')), parts along dimension 0, may hold values from 0.1 to 1
- expert_block: int32 [4], replicated, may hold values from 0 to 3, each once
- w_gate: bfloat16 [7168, 4096], P(None, ('node', 'local')), may hold values from -0.0625 to 0.0625
- w_up: bfloat16 [7168, 4096], P(None, ('node', 'local')), may hold values from -0.0625 to 0.0625
- w_down: bfloat16 [4096, 7168], P(('node', 'local')), may hold values from -0.1875 to 0.1875
Outputs:
- combined: bfloat16 [256, 7168], P(('groups', 'node', 'local')), parts along dimension 0
There are 2 independent parts, one for each index of `groups`. A program takes and returns all parts, laid end to end along the dimension named above; an argument that names none is the same for every part. Nothing has to cross between parts.
Inputs may be any that keep to these rules, and one draw needn't show every extreme that they name: `expert_ids`: each row names 2 different experts; among the rows of one device no expert is named by more than 6 pairs, and in every draw some device names some expert exactly 6 times. `expert_block`: A permutation of the experts.
All inputs are finite; a program needn't handle non-finite values.
Results may differ from a plain program's by a relative error of at most 0.0065.
Values may be sent and summed in bfloat16 or wider, within the bound.
A program may use at most 64 MiB of HBM per device.

v0:
```python
import jax
import jax.numpy as jnp
from jax import lax
from jax.sharding import PartitionSpec as P


def per_device(hidden_rows, expert_ids, gate_values, expert_block, w_gate, w_up, w_down):
    row_count, feature_width = hidden_rows.shape
    top_count = expert_ids.shape[1]
    experts = expert_block.shape[0]
    node_count = lax.axis_size("node")
    local_count = lax.axis_size("local")
    device_count = node_count * local_count
    capacity = row_count * top_count * 3 // (2 * experts)
    flat_ids = expert_ids.reshape(-1)
    onehot = (flat_ids[:, None] == jnp.arange(experts, dtype=jnp.int32)[None, :]).astype(jnp.int32)
    slot_index = jnp.sum((jnp.cumsum(onehot, axis=0) - onehot) * onehot, axis=1)
    target_block = jnp.sum(onehot * expert_block[None, :], axis=1)
    position = target_block * capacity + slot_index
    row_index = jnp.arange(row_count * top_count, dtype=jnp.int32) // top_count
    outgoing = (
        jnp.zeros((experts * capacity, feature_width), jnp.bfloat16)
        .at[position]
        .set(hidden_rows[row_index])
    )
    copies = jnp.repeat(outgoing.reshape(experts, capacity, feature_width), 4, axis=0)
    received = lax.all_to_all(
        copies, ("node", "local"), split_axis=0, concat_axis=0, tiled=True
    ).reshape(device_count * capacity, feature_width)
    gate_act = jnp.dot(received, w_gate, preferred_element_type=jnp.float32)
    up_act = jnp.dot(received, w_up, preferred_element_type=jnp.float32)
    hidden = (jax.nn.silu(gate_act) * up_act).astype(jnp.bfloat16)
    partial_out = jnp.dot(hidden, w_down, preferred_element_type=jnp.float32).astype(jnp.bfloat16)
    returned_all = lax.all_to_all(
        partial_out.reshape(device_count, capacity, feature_width),
        ("node", "local"),
        split_axis=0,
        concat_axis=0,
        tiled=True,
    )
    quarter_sum = jnp.sum(
        returned_all.reshape(experts, 4, capacity, feature_width).astype(jnp.float32), axis=1
    )
    expert_out = quarter_sum.astype(jnp.bfloat16).reshape(experts * capacity, feature_width)
    picked = expert_out[position].astype(jnp.float32).reshape(row_count, top_count, feature_width)
    combined = jnp.sum(picked * gate_values[:, :, None], axis=1)
    return combined.astype(jnp.bfloat16)


def solution(mesh):
    placed = (
        P(("groups", "node", "local"), None),
        P(("groups", "node", "local"), None),
        P(("groups", "node", "local"), None),
        P(),
        P(None, ("node", "local")),
        P(None, ("node", "local")),
        P(("node", "local"), None),
    )
    return jax.shard_map(
        per_device,
        mesh=mesh,
        in_specs=placed,
        out_specs=P(("groups", "node", "local"), None),
        check_vma=False,
    )
```

profile of v0, /device:TPU:15, one launch (start us, length us, event | category | flops | bytes accessed | tf_op | source)
XLA Modules:
  0.0 111.8 jit_solution(2082149386983993543)
XLA Ops:
  0.0 0.0 copy-start
  0.0 0.8 copy.10
  0.8 0.1 eq.15
  0.9 0.1 fusion.10
  1.0 0.8 select_reduce_fusion.1
  1.9 0.0 copy-done
  1.9 1.7 %scatter_custom_fusion = bf16[24,7168]{1,0:T(8,128)(2,1)S(1)} fusion(s32[16]{0:T(128)S(1)} %fusion.12, bf16[8,7168]{1,0:T(8,128)(2,1)S(1)} %copy-done, s32[1024]{0:T(1024)S(1)} %pad_clamp_fusion.1, bf16[]{:T(256)} %constant.28.clone.1), kind=kCustom, calls=%fused_computation.8 | custom fusion | bytes 344066 | tf_op jit(solution)/shard_map/scatter | solution.py:24
  3.5 0.1 reshape.94
  3.7 0.2 broadcast_in_dim.5
  3.8 48.0 %all_to_all.10 = bf16[16,6,7168]{2,1,0:T(8,128)(2,1)S(1)} all-to-all(bf16[16,6,7168]{2,1,0:T(8,128)(2,1)S(1)} %bitcast.14), channel_id=1, replica_groups=mesh['groups'=2,'node'=8,'local'=2] {'node','local'}, dimensions={0} | all-to-all | bytes 2752512 | tf_op jit(solution)/shard_map/all_to_all | solution.py:27
  51.9 0.5 reshape.96
  52.4 2.8 %fusion.14 = f32[96,256]{1,0:T(8,128)S(1)} fusion(bf16[96,7168]{1,0:T(8,128)(2,1)S(1)} %reshape.96, bf16[7168,256]{1,0:T(8,128)(2,1)} %param.11), kind=kOutput, calls=%fused_computation.32 | convolution fusion | flops 352321536 | bytes 5144576 | tf_op jit(solution)/shard_map/dot_general | solution.py:30
  55.2 5.3 %convolution_convert_fusion = bf16[96,7168]{1,0:T(8,128)(2,1)S(1)} fusion(bf16[256,7168]{1,0:T(8,128)(2,1)} %param.13, bf16[96,7168]{1,0:T(8,128)(2,1)S(1)} %reshape.96, bf16[7168,256]{1,0:T(8,128)(2,1)} %param.12, f32[96,256]{1,0:T(8,128)S(1)} %fusion.14), kind=kOutput, calls=%fused_computation.3 | convolution fusion | flops 705478656 | bytes 10190848 | tf_op jit(solution)/shard_map/dot_general | solution.py:33
  60.5 1.5 %reshape.97 = bf16[16,6,7168]{2,1,0:T(8,128)(2,1)} reshape(bf16[96,7168]{1,0:T(8,128)(2,1)S(1)} %convolution_convert_fusion) | data formatting | bytes 2752512 | tf_op jit(solution)/shard_map/reshape | solution.py:35
  62.0 0.0 copy-start.1
  62.0 5.2 %all-to-all-start.1 = ((bf16[16,6,7168]{2,1,0:T(8,128)(2,1)}), bf16[16,6,7168]{2,1,0:T(8,128)(2,1)S(1)}, u32[]{:S(2)}, u32[]{:S(2)}) async-start(bf16[16,6,7168]{2,1,0:T(8,128)(2,1)} %reshape.97), calls=%async_computation.1 | async-start | bytes 3670016 | tf_op jit(solution)/shard_map/all_to_all | solution.py:34
  67.2 0.0 copy-done.1
  67.2 0.1 copy.11
  67.3 41.7 %all-to-all-done.1 = bf16[16,6,7168]{2,1,0:T(8,128)(2,1)S(1)} async-done(((bf16[16,6,7168]{2,1,0:T(8,128)(2,1)}), bf16[16,6,7168]{2,1,0:T(8,128)(2,1)S(1)}, u32[]{:S(2)}, u32[]{:S(2)}) %all-to-all-start.1) | async-done | bytes 1376288 | tf_op jit(solution)/shard_map/all_to_all | solution.py:34
  109.0 0.4 bitcast_reduce_fusion
  109.4 0.1 reshape.99
  109.5 0.7 gather_fusion
  110.2 0.3 reshape.100
  110.5 1.3 %multiply_reduce_fusion = bf16[8,7168]{1,0:T(8,128)(2,1)} fusion(f32[8,2,7168]{2,1,0:T(2,128)S(1)} %reshape.100, f32[8,2]{1,0:T(8,128)S(1)} %copy.11), kind=kLoop, calls=%fused_computation.7 | loop fusion | flops 172032 | bytes 573504 | tf_op jit(solution)/shard_map/reduce_sum | solution.py:46
  (5 shorter events, 0.1 us)
Async XLA Ops:
  0.0 1.9 %copy-start = (bf16[8,7168]{1,0:T(8,128)(2,1)S(1)}, bf16[8,7168]{1,0:T(8,128)(2,1)}, u32[]{:S(2)}) copy-start(bf16[8,7168]{1,0:T(8,128)(2,1)} %param.7) | copy-start | bytes 344068
  62.0 5.2 %copy-start.1 = (f32[8,2]{0,1:T(2,128)S(1)}, f32[8,2]{0,1:T(2,128)}, u32[]{:S(2)}) copy-start(f32[8,2]{0,1:T(2,128)} %param.9) | copy-start | bytes 196
  62.0 47.0 %all-to-all-start.1 = ((bf16[16,6,7168]{2,1,0:T(8,128)(2,1)}), bf16[16,6,7168]{2,1,0:T(8,128)(2,1)S(1)}, u32[]{:S(2)}, u32[]{:S(2)}) async-start(bf16[16,6,7168]{2,1,0:T(8,128)(2,1)} %reshape.97), calls=%async_computation.1 | async-start | bytes 3670016 | tf_op jit(solution)/shard_map/all_to_all | solution.py:34
where the time goes:
time: 112 us
  blocking collectives  48 us (43%)
  waiting for transfers between devices  41.7 us (37%)
  matrix products  8.04 us (7%)
  local copies, waits for them, and re-layouts  6.08 us (5%)
  starting transfers between devices  5.22 us (5%)
  other arithmetic  2.63 us (2%)
    all_to_all x1, blocking collectives, per_device(): lax.all_to_all(copies, ('node', 'local'), split_axis=0, concat_axis=0, ti...  48 us
    all_to_all x1, waiting for transfers between devices, per_device(): lax.all_to_all(partial_out.reshape(device_count, capacity, feature_width)...  41.7 us
    dot_general x1, matrix products, per_device(): jnp.dot(hidden, w_down, preferred_element_type=jnp.float32)  5.28 us
    all_to_all x1, starting transfers between devices, per_device(): lax.all_to_all(partial_out.reshape(device_count, capacity, feature_width)...  5.22 us
    dot_general x1, matrix products, per_device(): gate_act = jnp.dot(received, w_gate, preferred_element_type=jnp.float32)  2.76 us
  transfers between devices with their start and end apart: 1, of which 1 were waited for; matrix products, arithmetic and copies ran while one was open for 0% of the time, Pallas kernels for 0%

commit v1 on v0

v1 whole, which is shorter than its diff:
```python
import functools
import jax
import jax.numpy as jnp
from jax import lax
from jax.experimental import pallas as pl
from jax.experimental.pallas import tpu as pltpu
from jax.sharding import PartitionSpec as P

MESH = pl.DeviceIdType.MESH
CHUNKS = 4


def routed_kernel(planes, ids_ref, gate_ref, block_ref, x_ref, wg_ref, wu_ref, wd_ref, out_ref,
                  w1, wd, xs, xr, cs, cr, rows_in, acc, ps, pr, ys, yr, keep, zs, zr, fs, fr,
                  w_sem, one_sem, chunk_send, chunk_recv, zin_send, zin_recv, zout_send, zout_recv):
    node, core = lax.axis_index("node"), lax.axis_index("local")
    plane, column = node // 2, node % 2
    row_count, width = x_ref.shape
    half = width // 2
    chunks = xs.shape[0]
    piece = half // chunks
    pair = 2 * row_count
    hidden_units = wg_ref.shape[1]
    other_core = 1 - core
    sibling = {"local": other_core}
    across = {"node": plane * 2 + (1 - column)}

    def plane_at(step):
        return {"node": lax.rem(plane + step, planes) * 2 + column}

    def start_of(rel, k):
        side = core if rel == 0 else other_core
        return pl.multiple_of(side * half + k * piece, 128)

    loads = {}
    for rel in range(2):
        for k in range(chunks):
            span = pl.ds(start_of(rel, k), piece)
            loads[0, rel, k] = pltpu.make_async_copy(
                wg_ref.at[span, :], w1.at[rel, k, :, pl.ds(0, hidden_units)], w_sem.at[0, rel, k])
            loads[1, rel, k] = pltpu.make_async_copy(
                wu_ref.at[span, :], w1.at[rel, k, :, pl.ds(hidden_units, hidden_units)], w_sem.at[1, rel, k])
            loads[2, rel, k] = pltpu.make_async_copy(wd_ref.at[:, span], wd.at[rel, k], w_sem.at[2, rel, k])
    for kind in ((0, 1), (2,)):
        for rel in range(2):
            for k in range(chunks):
                for which in kind:
                    loads[which, rel, k].start()

    barrier = pltpu.get_barrier_semaphore()
    partners = [sibling, across] + [plane_at(j) for j in range(1, planes)]
    for partner in partners:
        pl.semaphore_signal(barrier, inc=1, device_id=partner, device_id_type=MESH)

    for k in range(chunks):
        xs[k] = x_ref[:, pl.ds(start_of(1, k), piece)].astype(jnp.float32)
    ids = ids_ref[...]
    gates = gate_ref[...]
    target = jnp.zeros(ids.shape, jnp.int32)
    for e in range(block_ref.shape[0]):
        ahead = block_ref[e] - plane
        target = jnp.where(ids == e, jnp.where(ahead < 0, ahead + planes, ahead), target)
    lane = lax.broadcasted_iota(jnp.int32, cs.shape, 1)
    weight = jnp.zeros(cs.shape, jnp.float32)
    for k in range(ids.shape[1]):
        weight += jnp.where(target[:, k:k + 1] == lane, gates[:, k:k + 1], 0.0)
    cs[...] = weight

    pl.semaphore_wait(barrier, len(partners))

    sent = []

    def send(src, dst, send_sem, recv_sem, to):
        copy = pltpu.make_async_remote_copy(
            src_ref=src, dst_ref=dst, send_sem=send_sem, recv_sem=recv_sem, device_id=to, device_id_type=MESH)
        copy.start()
        sent.append(copy)
        return copy

    def by_chunk(kind, k, src, dst, to):
        return send(src, dst, chunk_send.at[kind, k], chunk_recv.at[kind, k], to)

    def in_order(own, other):
        return jnp.where(core == 0, jnp.concatenate([own, other], 0), jnp.concatenate([other, own], 0))

    swaps = [by_chunk(0, k, xs.at[k], xr.at[k], sibling) for k in range(chunks)]
    weights_swap = send(cs, cr, one_sem.at[0], one_sem.at[1], sibling)
    first, rest = pl.ds(0, pair), pl.ds(pair, (planes - 1) * pair)
    z_in, y_first, y_rest, b_first, b_rest, b_across = [], [], [], [], [], []
    for k in range(chunks):
        swaps[k].wait_recv()
        own = x_ref[:, pl.ds(start_of(0, k), piece)].astype(jnp.float32)
        rows_in[0, k, 0, first, :] = in_order(own, xr[k]).astype(jnp.bfloat16)
        mine = rows_in.at[0, k, 0, first, :]
        z_in.append([
            send(mine, rows_in.at[0, k, 0, pl.ds((planes - j) * pair, pair), :],
                 zin_send.at[k, planes - j], zin_recv.at[k, planes - j], plane_at(j))
            for j in range(1, planes)])
        y_first.append(by_chunk(1, k, mine, rows_in.at[0, k, 1, first, :], across))
        b_first.append(by_chunk(2, k, mine, rows_in.at[1, k, 0, first, :], sibling))

    acc[...] = jnp.zeros_like(acc)

    def pass_on(k):
        for copy in z_in[k]:
            copy.wait_recv()
        came = rows_in.at[0, k, 0, rest, :]
        y_rest.append(by_chunk(3, k, came, rows_in.at[0, k, 1, rest, :], across))
        b_rest.append(by_chunk(4, k, came, rows_in.at[1, k, 0, rest, :], sibling))

    def multiply(rel, k):
        loads[0, rel, k].wait()
        loads[1, rel, k].wait()
        lhs = rows_in[rel, k].reshape(2 * planes * pair, piece)
        acc[...] += jnp.dot(lhs, w1[rel, k], preferred_element_type=jnp.float32)

    def take_across(k):
        y_first[k].wait_recv()
        y_rest[k].wait_recv()
        b_across.append(by_chunk(5, k, rows_in.at[0, k, 1], rows_in.at[1, k, 1], sibling))
        multiply(0, k)

    def take_sibling(k):
        b_first[k].wait_recv()
        b_rest[k].wait_recv()
        b_across[k].wait_recv()
        multiply(1, k)

    for k in range(chunks + 2):
        if k < chunks:
            pass_on(k)
        if 1 <= k <= chunks:
            take_across(k - 1)
        if k >= 2:
            take_sibling(k - 2)

    gate_act = acc[:, :hidden_units]
    hidden = (gate_act / (1.0 + jnp.exp(-gate_act)) * acc[:, hidden_units:]).astype(jnp.bfloat16)
    weights_swap.wait_recv()
    weight = in_order(weight, cr[...])

    def part(rel, k):
        loads[2, rel, k].wait()
        return jnp.dot(hidden, wd[rel, k], preferred_element_type=jnp.float32)

    p_out, y_out, z_out, f_out = [], [], [], []

    def stage_a(k):
        ps[k] = part(1, k).astype(jnp.bfloat16)
        p_out.append(by_chunk(6, k, ps.at[k], pr.at[k], sibling))

    def stage_b(k):
        mine = part(0, k)
        p_out[k].wait_recv()
        total = mine + pr[k].astype(jnp.float32)
        ys[k] = total[planes * pair:].astype(jnp.bfloat16)
        y_out.append(by_chunk(7, k, ys.at[k], yr.at[k], across))
        keep[k] = total[:planes * pair]

    def stage_c(k):
        y_out[k].wait_recv()
        zs[k] = (keep[k] + yr[k].astype(jnp.float32)).astype(jnp.bfloat16)
        z_out.append([
            send(zs.at[k, pl.ds(j * pair, pair), :], zr.at[k, pl.ds((planes - j) * pair, pair), :],
                 zout_send.at[k, planes - j], zout_recv.at[k, planes - j], plane_at(j))
            for j in range(1, planes)])

    def stage_d(k):
        for copy in z_out[k]:
            copy.wait_recv()
        total = weight[:, 0:1] * zs[k, first, :].astype(jnp.float32)
        for s in range(1, planes):
            total += weight[:, s:s + 1] * zr[k, pl.ds(s * pair, pair), :].astype(jnp.float32)
        low, high = total[:row_count], total[row_count:]
        fs[k] = jnp.where(core == 0, high, low)
        f_out.append(by_chunk(8, k, fs.at[k], fr.at[k], sibling))
        out_ref[:, pl.ds(start_of(0, k), piece)] = jnp.where(core == 0, low, high)

    stage_a(0)
    for k in range(chunks):
        if k + 1 < chunks:
            stage_a(k + 1)
        stage_b(k)
    for k in range(chunks + 1):
        if k < chunks:
            stage_c(k)
        if k >= 1:
            stage_d(k - 1)
    for k in range(chunks):
        f_out[k].wait_recv()
        out_ref[:, pl.ds(start_of(1, k), piece)] = fr[k]
    for copy in sent:
        copy.wait_send()


def per_device(hidden_rows, expert_ids, gate_values, expert_block, w_gate, w_up, w_down):
    rows, width = hidden_rows.shape
    planes = lax.axis_size("node") // 2
    units = w_gate.shape[1]
    pair, chunks = 2 * rows, CHUNKS
    piece = width // 2 // chunks
    column = planes * pair
    bf16, f32 = jnp.bfloat16, jnp.float32
    vmem = pl.BlockSpec(memory_space=pltpu.VMEM)
    anywhere = pl.BlockSpec(memory_space=pl.ANY)
    dma = pltpu.SemaphoreType.DMA
    combined = pl.pallas_call(
        functools.partial(routed_kernel, planes),
        out_shape=jax.ShapeDtypeStruct((rows, width), f32),
        in_specs=[vmem, vmem, pl.BlockSpec(memory_space=pltpu.SMEM), vmem, anywhere, anywhere, anywhere],
        out_specs=vmem,
        scratch_shapes=[
            pltpu.VMEM((2, chunks, piece, 2 * units), bf16),
            pltpu.VMEM((2, chunks, units, piece), bf16),
            pltpu.VMEM((chunks, rows, piece), f32),
            pltpu.VMEM((chunks, rows, piece), f32),
            pltpu.VMEM((rows, 128), f32),
            pltpu.VMEM((rows, 128), f32),
            pltpu.VMEM((2, chunks, 2, column, piece), bf16),
            pltpu.VMEM((2 * column, 2 * units), f32),
            pltpu.VMEM((chunks, 2 * column, piece), bf16),
            pltpu.VMEM((chunks, 2 * column, piece), bf16),
            pltpu.VMEM((chunks, column, piece), bf16),
            pltpu.VMEM((chunks, column, piece), bf16),
            pltpu.VMEM((chunks, column, piece), f32),
            pltpu.VMEM((chunks, column, piece), bf16),
            pltpu.VMEM((chunks, column, piece), bf16),
            pltpu.VMEM((chunks, rows, piece), f32),
            pltpu.VMEM((chunks, rows, piece), f32),
            dma((3, 2, chunks)),
            dma((2,)),
            dma((9, chunks)),
            dma((9, chunks)),
            dma((chunks, planes)),
            dma((chunks, planes)),
            dma((chunks, planes)),
            dma((chunks, planes)),
        ],
        compiler_params=pltpu.CompilerParams(
            collective_id=0, has_side_effects=True, vmem_limit_bytes=56 * 1024 * 1024),
    )(expert_ids, gate_values, expert_block, hidden_rows, w_gate, w_up, w_down)
    return combined.astype(bf16)


def solution(mesh):
    placed = (
        P(("groups", "node", "local"), None),
        P(("groups", "node", "local"), None),
        P(("groups", "node", "local"), None),
        P(),
        P(None, ("node", "local")),
        P(None, ("node", "local")),
        P(("node", "local"), None),
    )
    return jax.shard_map(
        per_device,
        mesh=mesh,
        in_specs=placed,
        out_specs=P(("groups", "node", "local"), None),
        check_vma=False,
    )
```

time: 112 us -> 50.8 us (0.45)
  the two profiles are of different devices: /device:TPU:15 before, /device:TPU:0 now
where the time goes in v1:
time: 50.8 us; the launch traced here: 50.6 us
  Pallas kernels  46.4 us (91%)
  local copies, waits for them, and re-layouts  2.68 us (5%)
  other arithmetic  1.6 us (3%)
    pallas_call x1, Pallas kernels, per_device(): pl.pallas_call(functools.partial(routed_kernel, planes), out_shape=jax.Sh...  46.4 us
    unnamed x2, local copies, waits for them, and re-layouts  2.68 us
    convert_element_type x1, other arithmetic, per_device(): return combined.astype(bf16)  1.6 us

profile of v1, /device:TPU:0, one launch (start us, length us, event | category | flops | bytes accessed | tf_op | source)
XLA Modules:
  0.0 50.6 jit_solution(18165185205110239305)
XLA Ops:
  0.0 1.3 %copy.8.ids_ref = s32[8,2]{1,0:T(8,128)} copy(s32[8,2]{0,1:T(2,128)} %param.8) | data formatting | bytes 128 | tf_op args[1]
  1.3 1.3 %copy.9.gate_ref = f32[8,2]{1,0:T(8,128)} copy(f32[8,2]{0,1:T(2,128)} %param.9) | data formatting | bytes 128 | tf_op args[2]
  2.7 46.4 %shard_map.73 = f32[8,7168]{1,0:T(8,128)} custom-call(s32[8,2]{1,0:T(8,128)} %copy.8.ids_ref, f32[8,2]{1,0:T(8,128)} %copy.9.gate_ref, s32[4]{0:T(128)} %block_ref.1, bf16[8,7168]{1,0:T(8,128)(2,1)} %x_ref.1, bf16[7168,256]{1,0:T(8,128)(2,1)} %wg_ref.1, bf16[7168,256]{1,0:T(8,128)(2,1)} %wu_ref.1, bf16[256,7168]{1,0:T(8,128)(2,1)} %wd_ref.1), custom_call_target="tpu_custom_call" | custom-call | tf_op jit(solution)/shard_map/pallas_call | solution.py:207
  49.0 1.6 %convert_element_type.3 = bf16[8,7168]{1,0:T(8,128)(2,1)} convert(f32[8,7168]{1,0:T(8,128)} %shard_map.73) | non-fusion elementwise | flops 57344 | bytes 344064 | tf_op jit(solution)/shard_map/convert_element_type | solution.py:242

commit v2 on v1

v2 whole, which is shorter than its diff:
```python
import functools
import jax
import jax.numpy as jnp
from jax import lax
from jax.experimental import pallas as pl
from jax.experimental.pallas import tpu as pltpu
from jax.sharding import PartitionSpec as P

MESH = pl.DeviceIdType.MESH
CHUNKS = 4


def routed_kernel(planes, ids_ref, gate_ref, block_ref, x_ref, wg_ref, wu_ref, wd_ref, out_ref,
                  w1, wd, rows_in, acc, mine, ps, pr, ys, yr, keep, zs, zr,
                  w_sem, chunk_send, chunk_recv, zin_send, zin_recv, zout_send, zout_recv):
    node, core = lax.axis_index("node"), lax.axis_index("local")
    plane, column = node // 2, node % 2
    row_count, width = x_ref.shape
    half = width // 2
    chunks = ps.shape[0]
    piece = half // chunks
    pair = 2 * row_count
    hidden_units = wg_ref.shape[1]
    sibling = {"local": 1 - core}
    across = {"node": plane * 2 + (1 - column)}

    def plane_at(step):
        return {"node": lax.rem(plane + step, planes) * 2 + column}

    def span(side, k):
        return pl.ds(side * half + k * piece, piece)

    barrier = pltpu.get_barrier_semaphore()
    partners = [sibling, across] + [plane_at(j) for j in range(1, planes)]
    for partner in partners:
        pl.semaphore_signal(barrier, inc=1, device_id=partner, device_id_type=MESH)

    first, rest = pl.ds(0, pair), pl.ds(pair, (planes - 1) * pair)
    for k in range(chunks):
        packed = jnp.concatenate([x_ref[:, span(0, k)].astype(jnp.float32), x_ref[:, span(1, k)].astype(jnp.float32)], 0)
        rows_in[0, k, 0, first, :] = packed.astype(jnp.bfloat16)

    pl.semaphore_wait(barrier, len(partners))

    sent = []

    def send(src, dst, send_sem, recv_sem, to):
        copy = pltpu.make_async_remote_copy(
            src_ref=src, dst_ref=dst, send_sem=send_sem, recv_sem=recv_sem, device_id=to, device_id_type=MESH)
        copy.start()
        sent.append(copy)
        return copy

    def by_chunk(kind, k, src, dst, to):
        return send(src, dst, chunk_send.at[kind, k], chunk_recv.at[kind, k], to)

    z_in, y_first, y_rest, b_first, b_rest, b_across = [], [], [], [], [], []
    for k in range(chunks):
        own = rows_in.at[0, k, 0, first, :]
        z_in.append([
            send(own, rows_in.at[0, k, 0, pl.ds((planes - j) * pair, pair), :],
                 zin_send.at[k, planes - j], zin_recv.at[k, planes - j], plane_at(j))
            for j in range(1, planes)])
        y_first.append(by_chunk(1, k, own, rows_in.at[0, k, 1, first, :], across))
        b_first.append(by_chunk(2, k, own, rows_in.at[1, k, 0, first, :], sibling))

    loads = {}
    for side in range(2):
        for k in range(chunks):
            loads[0, side, k] = pltpu.make_async_copy(
                wg_ref.at[span(side, k), :], w1.at[side, k, :, pl.ds(0, hidden_units)], w_sem.at[0, side, k])
            loads[1, side, k] = pltpu.make_async_copy(
                wu_ref.at[span(side, k), :], w1.at[side, k, :, pl.ds(hidden_units, hidden_units)], w_sem.at[1, side, k])
            loads[2, side, k] = pltpu.make_async_copy(wd_ref.at[:, span(side, k)], wd.at[side, k], w_sem.at[2, side, k])
    for kinds in ((0, 1), (2,)):
        for k in range(chunks):
            for side in range(2):
                for kind in kinds:
                    loads[kind, side, k].start()

    ids = ids_ref[...]
    gates = gate_ref[...]
    target = jnp.zeros(ids.shape, jnp.int32)
    for e in range(block_ref.shape[0]):
        ahead = block_ref[e] - plane
        target = jnp.where(ids == e, jnp.where(ahead < 0, ahead + planes, ahead), target)
    square = (row_count, row_count)
    diagonal = lax.broadcasted_iota(jnp.int32, square, 0) == lax.broadcasted_iota(jnp.int32, square, 1)
    weights = []
    for s in range(planes):
        line = jnp.sum(jnp.where(target == s, gates, 0.0), axis=0, keepdims=True)
        upright = jnp.sum(jnp.where(diagonal, jnp.broadcast_to(line, square), 0.0), axis=1, keepdims=True)
        weights.append(jnp.concatenate([upright, upright], 0))

    acc[...] = jnp.zeros_like(acc)

    def pass_on(k):
        for copy in z_in[k]:
            copy.wait_recv()
        came = rows_in.at[0, k, 0, rest, :]
        y_rest.append(by_chunk(3, k, came, rows_in.at[0, k, 1, rest, :], across))
        b_rest.append(by_chunk(4, k, came, rows_in.at[1, k, 0, rest, :], sibling))

    def take_across(k):
        y_first[k].wait_recv()
        y_rest[k].wait_recv()
        b_across.append(by_chunk(5, k, rows_in.at[0, k, 1], rows_in.at[1, k, 1], sibling))

    def multiply(k):
        b_first[k].wait_recv()
        b_rest[k].wait_recv()
        b_across[k].wait_recv()
        loose = []
        for c in range(2):
            loose.append(rows_in[c, k].reshape(2 * planes, pair, piece).astype(jnp.float32))
        for side in range(2):
            loads[0, side, k].wait()
            loads[1, side, k].wait()
            lhs = jnp.concatenate([
                part[:, side * row_count:(side + 1) * row_count].reshape(planes * pair, piece) for part in loose], 0)
            acc[...] += jnp.dot(lhs.astype(jnp.bfloat16), w1[side, k], preferred_element_type=jnp.float32)

    for k in range(chunks + 2):
        if k < chunks:
            pass_on(k)
        if 1 <= k <= chunks:
            take_across(k - 1)
        if k >= 2:
            multiply(k - 2)

    gate_act = acc[:, :hidden_units]
    hidden = (gate_act / (1.0 + jnp.exp(-gate_act)) * acc[:, hidden_units:]).astype(jnp.bfloat16)

    p_out, y_out, z_out = [], [], []
    groups = 4 * planes

    def stage_a(k):
        sides = []
        for side in range(2):
            loads[2, side, k].wait()
            product = jnp.dot(hidden, wd[side, k], preferred_element_type=jnp.float32)
            sides.append(product.reshape(groups, row_count, piece))
        both = jnp.concatenate(sides, 1).reshape(groups * pair, piece)
        ps[k] = both[groups // 2 * pair:].astype(jnp.bfloat16)
        p_out.append(by_chunk(6, k, ps.at[k], pr.at[k], sibling))
        mine[k] = both[:groups // 2 * pair]

    def stage_b(k):
        p_out[k].wait_recv()
        total = mine[k] + pr[k].astype(jnp.float32)
        ys[k] = total[planes * pair:].astype(jnp.bfloat16)
        y_out.append(by_chunk(7, k, ys.at[k], yr.at[k], across))
        keep[k] = total[:planes * pair]

    def stage_c(k):
        y_out[k].wait_recv()
        zs[k] = (keep[k] + yr[k].astype(jnp.float32)).astype(jnp.bfloat16)
        z_out.append([
            send(zs.at[k, pl.ds(j * pair, pair), :], zr.at[k, pl.ds((planes - j) * pair, pair), :],
                 zout_send.at[k, planes - j], zout_recv.at[k, planes - j], plane_at(j))
            for j in range(1, planes)])

    def stage_d(k):
        for copy in z_out[k]:
            copy.wait_recv()
        total = weights[0] * zs[k, first, :].astype(jnp.float32)
        for s in range(1, planes):
            total += weights[s] * zr[k, pl.ds(s * pair, pair), :].astype(jnp.float32)
        out_ref[:, span(0, k)] = total[:row_count]
        out_ref[:, span(1, k)] = total[row_count:]

    stage_a(0)
    stage_a(1)
    for k in range(chunks):
        if k + 2 < chunks:
            stage_a(k + 2)
        stage_b(k)
    for k in range(chunks + 2):
        if k < chunks:
            stage_c(k)
        if k >= 2:
            stage_d(k - 2)
    for copy in sent:
        copy.wait_send()


def per_device(hidden_rows, expert_ids, gate_values, expert_block, w_gate, w_up, w_down):
    rows, width = hidden_rows.shape
    planes = lax.axis_size("node") // 2
    units = w_gate.shape[1]
    pair, chunks = 2 * rows, CHUNKS
    piece = width // 2 // chunks
    column = planes * pair
    bf16, f32 = jnp.bfloat16, jnp.float32
    vmem = pl.BlockSpec(memory_space=pltpu.VMEM)
    anywhere = pl.BlockSpec(memory_space=pl.ANY)
    dma = pltpu.SemaphoreType.DMA
    combined = pl.pallas_call(
        functools.partial(routed_kernel, planes),
        out_shape=jax.ShapeDtypeStruct((rows, width), f32),
        in_specs=[vmem, vmem, pl.BlockSpec(memory_space=pltpu.SMEM), vmem, anywhere, anywhere, anywhere],
        out_specs=vmem,
        scratch_shapes=[
            pltpu.VMEM((2, chunks, piece, 2 * units), bf16),
            pltpu.VMEM((2, chunks, units, piece), bf16),
            pltpu.VMEM((2, chunks, 2, column, piece), bf16),
            pltpu.VMEM((2 * column, 2 * units), f32),
            pltpu.VMEM((chunks, 2 * column, piece), f32),
            pltpu.VMEM((chunks, 2 * column, piece), bf16),
            pltpu.VMEM((chunks, 2 * column, piece), bf16),
            pltpu.VMEM((chunks, column, piece), bf16),
            pltpu.VMEM((chunks, column, piece), bf16),
            pltpu.VMEM((chunks, column, piece), f32),
            pltpu.VMEM((chunks, column, piece), bf16),
            pltpu.VMEM((chunks, column, piece), bf16),
            dma((3, 2, chunks)),
            dma((8, chunks)),
            dma((8, chunks)),
            dma((chunks, planes)),
            dma((chunks, planes)),
            dma((chunks, planes)),
            dma((chunks, planes)),
        ],
        compiler_params=pltpu.CompilerParams(
            collective_id=0, has_side_effects=True, vmem_limit_bytes=56 * 1024 * 1024),
    )(expert_ids.T, gate_values.T, expert_block, hidden_rows, w_gate, w_up, w_down)
    return combined.astype(bf16)


def solution(mesh):
    placed = (
        P(("groups", "node", "local"), None),
        P(("groups", "node", "local"), None),
        P(("groups", "node", "local"), None),
        P(),
        P(None, ("node", "local")),
        P(None, ("node", "local")),
        P(("node", "local"), None),
    )
    return jax.shard_map(
        per_device,
        mesh=mesh,
        in_specs=placed,
        out_specs=P(("groups", "node", "local"), None),
        check_vma=False,
    )
```

time: 50.8 us -> 46.6 us (0.917)
  local copies, waits for them, and re-layouts: 2.68 us -> 0 us
  Pallas kernels: 46.4 us -> 44.9 us
    unnamed x2 -> x0, local copies, waits for them, and re-layouts: 2.68 us -> none
    pallas_call x1, Pallas kernels: 46.4 us -> 44.9 us  [per_device(): pl.pallas_call(functools.partial(routed_kernel, planes), out_shape=jax.Sh...]
where the time goes in v2:
time: 46.6 us; the launch traced here: 46.5 us
  Pallas kernels  44.9 us (96%)
  other arithmetic  1.6 us (3%)
    pallas_call x1, Pallas kernels, per_device(): pl.pallas_call(functools.partial(routed_kernel, planes), out_shape=jax.Sh...  44.9 us
    convert_element_type x1, other arithmetic, per_device(): return combined.astype(bf16)  1.6 us

profile of v2, /device:TPU:0, one launch (start us, length us, event | category | flops | bytes accessed | tf_op | source)
XLA Modules:
  0.0 46.5 jit_solution(10816589449681945888)
XLA Ops:
  0.0 44.9 %shard_map.73 = f32[8,7168]{1,0:T(8,128)} custom-call(s32[2,8]{1,0:T(2,128)} %bitcast.2, f32[2,8]{1,0:T(2,128)} %bitcast.3, s32[4]{0:T(128)} %block_ref.1, bf16[8,7168]{1,0:T(8,128)(2,1)} %x_ref.1, bf16[7168,256]{1,0:T(8,128)(2,1)} %wg_ref.1, bf16[7168,256]{1,0:T(8,128)(2,1)} %wu_ref.1, bf16[256,7168]{1,0:T(8,128)(2,1)} %wd_ref.1), custom_call_target="tpu_custom_call" | custom-call | tf_op jit(solution)/shard_map/pallas_call | solution.py:198
  44.9 1.6 %convert_element_type.3 = bf16[8,7168]{1,0:T(8,128)(2,1)} convert(f32[8,7168]{1,0:T(8,128)} %shard_map.73) | non-fusion elementwise | flops 57344 | bytes 344064 | tf_op jit(solution)/shard_map/convert_element_type | solution.py:227

commit v3 on v2

v3 whole, which is shorter than its diff:
```python
import functools
import jax
import jax.numpy as jnp
from jax import lax
from jax.experimental import pallas as pl
from jax.experimental.pallas import tpu as pltpu
from jax.sharding import PartitionSpec as P

MESH = pl.DeviceIdType.MESH
PIECES = 8


def lane_spans(piece):
    cut = -(-piece // 256) * 128
    return [(0, cut), (cut, piece - cut)]


def routed_kernel(planes, capacity, ids_ref, gate_ref, block_ref, x_ref, wg_ref, wu_ref, wd_ref, out_ref,
                  w1, wd, xsend, rows_in, loose, acc, product, ps, pr, ys, yr, keep, zs, zr,
                  w_sem, chunk_send, chunk_recv, zin_send, zin_recv, zout_send, zout_recv):
    node, core = lax.axis_index("node"), lax.axis_index("local")
    plane, column = node // 2, node % 2
    row_count, width = x_ref.shape
    piece = width // PIECES
    spans = lane_spans(piece)
    chunks = len(spans)
    pair = capacity * PIECES
    column_rows = planes * pair
    hidden_units = wg_ref.shape[1]
    f32, bf16 = jnp.float32, jnp.bfloat16
    sibling = {"local": 1 - core}
    across = {"node": plane * 2 + (1 - column)}

    def plane_at(step):
        return {"node": lax.rem(plane + step, planes) * 2 + column}

    def lanes(k):
        return pl.ds(*spans[k])

    def at_piece(p, k):
        return pl.ds(p * piece + spans[k][0], spans[k][1])

    barrier = pltpu.get_barrier_semaphore()
    partners = [sibling, across] + [plane_at(j) for j in range(1, planes)]
    for partner in partners:
        pl.semaphore_signal(barrier, inc=1, device_id=partner, device_id_type=MESH)

    first, rest = pl.ds(0, pair), pl.ds(pair, (planes - 1) * pair)

    loads = {}
    for k in range(chunks):
        for p in range(PIECES):
            here = at_piece(p, k)
            loads[0, p, k] = pltpu.make_async_copy(
                wg_ref.at[here, :], w1.at[here, pl.ds(0, hidden_units)], w_sem.at[0, p, k])
            loads[1, p, k] = pltpu.make_async_copy(
                wu_ref.at[here, :], w1.at[here, pl.ds(hidden_units, hidden_units)], w_sem.at[1, p, k])
            loads[2, p, k] = pltpu.make_async_copy(wd_ref.at[:, here], wd.at[:, here], w_sem.at[2, p, k])
            loads[0, p, k].start()
            loads[1, p, k].start()
    for k in range(chunks):
        for p in range(PIECES):
            loads[2, p, k].start()

    def iota(shape, dim):
        return lax.broadcasted_iota(jnp.int32, shape, dim)

    def exact_dot(a, b):
        return jnp.dot(a.astype(f32).astype(bf16), b.astype(f32).astype(bf16), preferred_element_type=f32)

    ids = ids_ref[...]
    gates = gate_ref[...]
    target = jnp.zeros(ids.shape, jnp.int32)
    for e in range(block_ref.shape[0]):
        ahead = block_ref[e] - plane
        target = jnp.where(ids == e, jnp.where(ahead < 0, ahead + planes, ahead), target)
    table = (planes, row_count)
    named = jnp.zeros(table, f32)
    for c in range(ids.shape[0]):
        named += jnp.where(jnp.broadcast_to(target[c:c + 1], table) == iota(table, 0), 1.0, 0.0)
    square = (row_count, row_count)
    before = exact_dot(named, jnp.where(iota(square, 0) < iota(square, 1), 1.0, 0.0))
    place = jnp.where(named > 0.5, before + (capacity * iota(table, 0)).astype(f32), 250.0)
    spread = (planes * capacity, planes)
    offset = iota(spread, 0) - capacity * iota(spread, 1)
    expand = jnp.where((offset >= 0) & (offset < capacity), 1.0, 0.0)
    grid = (planes * capacity, row_count)
    hits = jnp.where(exact_dot(expand, place) == iota(grid, 0).astype(f32), 1.0, 0.0)
    wide = (row_count, PIECES * row_count)
    hits = exact_dot(hits, jnp.where(iota(wide, 1) % row_count == iota(wide, 0), 1.0, 0.0))
    tall = (column_rows, planes * capacity)
    hits = exact_dot(jnp.where(iota(tall, 0) // PIECES == iota(tall, 1), 1.0, 0.0), hits)
    full = (column_rows, PIECES * row_count)
    choose = jnp.where(iota(full, 0) % PIECES == iota(full, 1) // row_count, hits, 0.0).astype(bf16)

    first, rest = pl.ds(0, pair), pl.ds(pair, column_rows - pair)
    for k in range(chunks):
        packed = jnp.concatenate([x_ref[:, at_piece(p, k)].astype(f32) for p in range(PIECES)], 0).astype(bf16)
        chosen = jnp.dot(choose, packed, preferred_element_type=f32).astype(bf16)
        xsend[:, lanes(k)] = chosen
        rows_in[0, 0, first, lanes(k)] = chosen[:pair]

    pl.semaphore_wait(barrier, len(partners))

    sent = []

    def send(src, dst, send_sem, recv_sem, to):
        copy = pltpu.make_async_remote_copy(
            src_ref=src, dst_ref=dst, send_sem=send_sem, recv_sem=recv_sem, device_id=to, device_id_type=MESH)
        copy.start()
        sent.append(copy)
        return copy

    def by_chunk(kind, k, src, dst, to):
        return send(src, dst, chunk_send.at[kind, k], chunk_recv.at[kind, k], to)

    z_in, y_first, y_rest, b_first, b_rest, b_across = [], [], [], [], [], []
    for k in range(chunks):
        z_in.append([
            send(xsend.at[pl.ds(j * pair, pair), lanes(k)],
                 rows_in.at[0, 0, pl.ds((planes - j) * pair, pair), lanes(k)],
                 zin_send.at[k, planes - j], zin_recv.at[k, planes - j], plane_at(j))
            for j in range(1, planes)])
        own = rows_in.at[0, 0, first, lanes(k)]
        y_first.append(by_chunk(1, k, own, rows_in.at[0, 1, first, lanes(k)], across))
        b_first.append(by_chunk(2, k, own, rows_in.at[1, 0, first, lanes(k)], sibling))

    diagonal = iota(square, 0) == iota(square, 1)
    weights = []
    for s in range(planes):
        line = jnp.sum(jnp.where(target == s, gates, 0.0), axis=0, keepdims=True)
        upright = jnp.sum(jnp.where(diagonal, jnp.broadcast_to(line, square), 0.0), axis=1, keepdims=True)
        weights.append(jnp.concatenate([upright] * PIECES, 0))

    acc[...] = jnp.zeros_like(acc)
    block_rows = 4 * planes * capacity

    def pass_on(k):
        for copy in z_in[k]:
            copy.wait_recv()
        came = rows_in.at[0, 0, rest, lanes(k)]
        y_rest.append(by_chunk(3, k, came, rows_in.at[0, 1, rest, lanes(k)], across))
        b_rest.append(by_chunk(4, k, came, rows_in.at[1, 0, rest, lanes(k)], sibling))

    def take_across(k):
        y_first[k].wait_recv()
        y_rest[k].wait_recv()
        b_across.append(by_chunk(5, k, rows_in.at[0, 1, :, lanes(k)], rows_in.at[1, 1, :, lanes(k)], sibling))

    def multiply(k):
        b_first[k].wait_recv()
        b_rest[k].wait_recv()
        b_across[k].wait_recv()
        start, size = spans[k]
        for t in range(size // 128):
            tile = rows_in[:, :, :, pl.ds(start + t * 128, 128)]
            loose[t] = tile.reshape(4 * column_rows, 128).astype(f32)
        for p in range(PIECES):
            loads[0, p, k].wait()
            loads[1, p, k].wait()
            lhs = jnp.concatenate([
                loose[t, pl.ds(p, block_rows, stride=PIECES), :] for t in range(size // 128)], 1)
            acc[...] += jnp.dot(lhs.astype(bf16), w1[at_piece(p, k), :], preferred_element_type=f32)

    for k in range(chunks):
        pass_on(k)
        if k >= 1:
            take_across(k - 1)
    take_across(chunks - 1)
    for k in range(chunks):
        multiply(k)

    gate_act = acc[:, :hidden_units]
    hidden = (gate_act / (1.0 + jnp.exp(-gate_act)) * acc[:, hidden_units:]).astype(bf16)

    p_out, y_out, z_out = [], [], []

    def stage_a(k):
        start, size = spans[k]
        for p in range(PIECES):
            loads[2, p, k].wait()
            result = jnp.dot(hidden, wd[:, at_piece(p, k)], preferred_element_type=f32)
            for t in range(size // 128):
                product[start // 128 + t, pl.ds(p, block_rows, stride=PIECES), :] = result[:, t * 128:(t + 1) * 128]
        for t in range(size // 128):
            ps[:, pl.ds(start + t * 128, 128)] = product[
                start // 128 + t, pl.ds(2 * column_rows, 2 * column_rows), :].astype(bf16)
        p_out.append(by_chunk(6, k, ps.at[:, lanes(k)], pr.at[:, lanes(k)], sibling))

    def stage_b(k):
        p_out[k].wait_recv()
        start, size = spans[k]
        for t in range(size // 128):
            here = pl.ds(start + t * 128, 128)
            total = product[start // 128 + t, pl.ds(0, 2 * column_rows), :] + pr[:, here].astype(f32)
            ys[:, here] = total[column_rows:].astype(bf16)
            keep[:, here] = total[:column_rows]
        y_out.append(by_chunk(7, k, ys.at[:, lanes(k)], yr.at[:, lanes(k)], across))

    def stage_c(k):
        y_out[k].wait_recv()
        zs[:, lanes(k)] = (keep[:, lanes(k)] + yr[:, lanes(k)].astype(f32)).astype(bf16)
        z_out.append([
            send(zs.at[pl.ds(j * pair, pair), lanes(k)], zr.at[pl.ds((planes - j) * pair, pair), lanes(k)],
                 zout_send.at[k, planes - j], zout_recv.at[k, planes - j], plane_at(j))
            for j in range(1, planes)])

    def stage_d(k):
        for copy in z_out[k]:
            copy.wait_recv()
        total = None
        for s in range(planes):
            block = zs[first, lanes(k)] if s == 0 else zr[pl.ds(s * pair, pair), lanes(k)]
            picked = lax.dot_general(
                choose[s * pair:(s + 1) * pair], block, (((0,), (0,)), ((), ())), preferred_element_type=f32)
            total = weights[s] * picked if s == 0 else total + weights[s] * picked
        for p in range(PIECES):
            out_ref[:, at_piece(p, k)] = total[p * row_count:(p + 1) * row_count]

    for k in range(chunks):
        stage_a(k)
        if k >= 1:
            stage_b(k - 1)
    stage_b(chunks - 1)
    for k in range(chunks):
        stage_c(k)
    for k in range(chunks):
        stage_d(k)
    for copy in sent:
        copy.wait_send()


def per_device(hidden_rows, expert_ids, gate_values, expert_block, w_gate, w_up, w_down):
    rows, width = hidden_rows.shape
    planes = lax.axis_size("node") // 2
    units = w_gate.shape[1]
    capacity = rows * expert_ids.shape[1] * 3 // (2 * expert_block.shape[0])
    pair = capacity * PIECES
    piece = width // PIECES
    chunks = len(lane_spans(piece))
    largest = max(size for _, size in lane_spans(piece))
    column = planes * pair
    bf16, f32 = jnp.bfloat16, jnp.float32
    vmem = pl.BlockSpec(memory_space=pltpu.VMEM)
    anywhere = pl.BlockSpec(memory_space=pl.ANY)
    dma = pltpu.SemaphoreType.DMA
    combined = pl.pallas_call(
        functools.partial(routed_kernel, planes, capacity),
        out_shape=jax.ShapeDtypeStruct((rows, width), f32),
        in_specs=[vmem, vmem, pl.BlockSpec(memory_space=pltpu.SMEM), vmem, anywhere, anywhere, anywhere],
        out_specs=vmem,
        scratch_shapes=[
            pltpu.VMEM((width, 2 * units), bf16),
            pltpu.VMEM((units, width), bf16),
            pltpu.VMEM((column, piece), bf16),
            pltpu.VMEM((2, 2, column, piece), bf16),
            pltpu.VMEM((largest // 128, 4 * column, 128), f32),
            pltpu.VMEM((4 * planes * capacity, 2 * units), f32),
            pltpu.VMEM((piece // 128, 4 * column, 128), f32),
            pltpu.VMEM((2 * column, piece), bf16),
            pltpu.VMEM((2 * column, piece), bf16),
            pltpu.VMEM((column, piece), bf16),
            pltpu.VMEM((column, piece), bf16),
            pltpu.VMEM((column, piece), f32),
            pltpu.VMEM((column, piece), bf16),
            pltpu.VMEM((column, piece), bf16),
            dma((3, PIECES, chunks)),
            dma((8, chunks)),
            dma((8, chunks)),
            dma((chunks, planes)),
            dma((chunks, planes)),
            dma((chunks, planes)),
            dma((chunks, planes)),
        ],
        compiler_params=pltpu.CompilerParams(
            collective_id=0, has_side_effects=True, vmem_limit_bytes=56 * 1024 * 1024),
    )(expert_ids.T, gate_values.T, expert_block, hidden_rows, w_gate, w_up, w_down)
    return combined.astype(bf16)


def solution(mesh):
    placed = (
        P(("groups", "node", "local"), None),
        P(("groups", "node", "local"), None),
        P(("groups", "node", "local"), None),
        P(),
        P(None, ("node", "local")),
        P(None, ("node", "local")),
        P(("node", "local"), None),
    )
    return jax.shard_map(
        per_device,
        mesh=mesh,
        in_specs=placed,
        out_specs=P(("groups", "node", "local"), None),
        check_vma=False,
    )
```

time: 46.6 us -> 42.1 us (0.903)
  Pallas kernels: 44.9 us -> 40.4 us
    pallas_call x1, Pallas kernels: 44.9 us -> 40.4 us  [per_device(): pl.pallas_call(functools.partial(routed_kernel, planes, capacity), out_sh...]
where the time goes in v3:
time: 42.1 us; the launch traced here: 42 us
  Pallas kernels  40.4 us (96%)
  other arithmetic  1.6 us (4%)
    pallas_call x1, Pallas kernels, per_device(): pl.pallas_call(functools.partial(routed_kernel, planes, capacity), out_sh...  40.4 us
    convert_element_type x1, other arithmetic, per_device(): return combined.astype(bf16)  1.6 us

profile of v3, /device:TPU:0, one launch (start us, length us, event | category | flops | bytes accessed | tf_op | source)
XLA Modules:
  0.0 42.0 jit_solution(15582285051547919304)
XLA Ops:
  0.0 40.4 %shard_map.73 = f32[8,7168]{1,0:T(8,128)} custom-call(s32[2,8]{1,0:T(2,128)} %bitcast.2, f32[2,8]{1,0:T(2,128)} %bitcast.3, s32[4]{0:T(128)} %block_ref.1, bf16[8,7168]{1,0:T(8,128)(2,1)} %x_ref.1, bf16[7168,256]{1,0:T(8,128)(2,1)} %wg_ref.1, bf16[7168,256]{1,0:T(8,128)(2,1)} %wu_ref.1, bf16[256,7168]{1,0:T(8,128)(2,1)} %wd_ref.1), custom_call_target="tpu_custom_call" | custom-call | tf_op jit(solution)/shard_map/pallas_call | solution.py:247
  40.4 1.6 %convert_element_type.3 = bf16[8,7168]{1,0:T(8,128)(2,1)} convert(f32[8,7168]{1,0:T(8,128)} %shard_map.73) | non-fusion elementwise | flops 57344 | bytes 344064 | tf_op jit(solution)/shard_map/convert_element_type | solution.py:278

commit v4 on v3

--- a/solution.py
+++ b/solution.py
@@ -11,7 +11,7 @@
 
 
 def lane_spans(piece):
-    cut = -(-piece // 256) * 128
+    cut = piece // 256 * 128
     return [(0, cut), (cut, piece - cut)]
 
 
@@ -47,20 +47,12 @@
 
     first, rest = pl.ds(0, pair), pl.ds(pair, (planes - 1) * pair)
 
-    loads = {}
-    for k in range(chunks):
-        for p in range(PIECES):
-            here = at_piece(p, k)
-            loads[0, p, k] = pltpu.make_async_copy(
-                wg_ref.at[here, :], w1.at[here, pl.ds(0, hidden_units)], w_sem.at[0, p, k])
-            loads[1, p, k] = pltpu.make_async_copy(
-                wu_ref.at[here, :], w1.at[here, pl.ds(hidden_units, hidden_units)], w_sem.at[1, p, k])
-            loads[2, p, k] = pltpu.make_async_copy(wd_ref.at[:, here], wd.at[:, here], w_sem.at[2, p, k])
-            loads[0, p, k].start()
-            loads[1, p, k].start()
-    for k in range(chunks):
-        for p in range(PIECES):
-            loads[2, p, k].start()
+    loads = [
+        pltpu.make_async_copy(wg_ref, w1.at[:, pl.ds(0, hidden_units)], w_sem.at[0]),
+        pltpu.make_async_copy(wu_ref, w1.at[:, pl.ds(hidden_units, hidden_units)], w_sem.at[1]),
+        pltpu.make_async_copy(wd_ref, wd, w_sem.at[2])]
+    for load in loads:
+        load.start()
 
     def iota(shape, dim):
         return lax.broadcasted_iota(jnp.int32, shape, dim)
@@ -114,7 +106,7 @@
     def by_chunk(kind, k, src, dst, to):
         return send(src, dst, chunk_send.at[kind, k], chunk_recv.at[kind, k], to)
 
-    z_in, y_first, y_rest, b_first, b_rest, b_across = [], [], [], [], [], []
+    z_in, y_first, y_rest, b_rest, b_across = [], [], [], [], []
     for k in range(chunks):
         z_in.append([
             send(xsend.at[pl.ds(j * pair, pair), lanes(k)],
@@ -123,7 +115,6 @@
             for j in range(1, planes)])
         own = rows_in.at[0, 0, first, lanes(k)]
         y_first.append(by_chunk(1, k, own, rows_in.at[0, 1, first, lanes(k)], across))
-        b_first.append(by_chunk(2, k, own, rows_in.at[1, 0, first, lanes(k)], sibling))
 
     diagonal = iota(square, 0) == iota(square, 1)
     weights = []
@@ -140,7 +131,7 @@
             copy.wait_recv()
         came = rows_in.at[0, 0, rest, lanes(k)]
         y_rest.append(by_chunk(3, k, came, rows_in.at[0, 1, rest, lanes(k)], across))
-        b_rest.append(by_chunk(4, k, came, rows_in.at[1, 0, rest, lanes(k)], sibling))
+        b_rest.append(by_chunk(2, k, rows_in.at[0, 0, :, lanes(k)], rows_in.at[1, 0, :, lanes(k)], sibling))
 
     def take_across(k):
         y_first[k].wait_recv()
@@ -148,7 +139,6 @@
         b_across.append(by_chunk(5, k, rows_in.at[0, 1, :, lanes(k)], rows_in.at[1, 1, :, lanes(k)], sibling))
 
     def multiply(k):
-        b_first[k].wait_recv()
         b_rest[k].wait_recv()
         b_across[k].wait_recv()
         start, size = spans[k]
@@ -156,8 +146,6 @@
             tile = rows_in[:, :, :, pl.ds(start + t * 128, 128)]
             loose[t] = tile.reshape(4 * column_rows, 128).astype(f32)
         for p in range(PIECES):
-            loads[0, p, k].wait()
-            loads[1, p, k].wait()
             lhs = jnp.concatenate([
                 loose[t, pl.ds(p, block_rows, stride=PIECES), :] for t in range(size // 128)], 1)
             acc[...] += jnp.dot(lhs.astype(bf16), w1[at_piece(p, k), :], preferred_element_type=f32)
@@ -167,6 +155,8 @@
         if k >= 1:
             take_across(k - 1)
     take_across(chunks - 1)
+    for load in loads:
+        load.wait()
     for k in range(chunks):
         multiply(k)
 
@@ -178,7 +168,6 @@
     def stage_a(k):
         start, size = spans[k]
         for p in range(PIECES):
-            loads[2, p, k].wait()
             result = jnp.dot(hidden, wd[:, at_piece(p, k)], preferred_element_type=f32)
             for t in range(size // 128):
                 product[start // 128 + t, pl.ds(p, block_rows, stride=PIECES), :] = result[:, t * 128:(t + 1) * 128]
@@ -264,7 +253,7 @@
             pltpu.VMEM((column, piece), f32),
             pltpu.VMEM((column, piece), bf16),
             pltpu.VMEM((column, piece), bf16),
-            dma((3, PIECES, chunks)),
+            dma((3,)),
             dma((8, chunks)),
             dma((8, chunks)),
             dma((chunks, planes)),

time: 42.1 us -> 39.6 us (0.941)
  Pallas kernels: 40.4 us -> 37.8 us
    pallas_call x1, Pallas kernels: 40.4 us -> 37.8 us  [per_device(): pl.pallas_call(functools.partial(routed_kernel, planes, capacity), out_sh...]
where the time goes in v4:
time: 39.6 us; the launch traced here: 39.4 us
  Pallas kernels  37.8 us (95%)
  other arithmetic  1.6 us (4%)
    pallas_call x1, Pallas kernels, per_device(): pl.pallas_call(functools.partial(routed_kernel, planes, capacity), out_sh...  37.8 us
    convert_element_type x1, other arithmetic, per_device(): return combined.astype(bf16)  1.6 us

profile of v4, /device:TPU:0, one launch (start us, length us, event | category | flops | bytes accessed | tf_op | source)
XLA Modules:
  0.0 39.4 jit_solution(6666643996551509364)
XLA Ops:
  0.0 37.8 %shard_map.73 = f32[8,7168]{1,0:T(8,128)} custom-call(s32[2,8]{1,0:T(2,128)} %bitcast.2, f32[2,8]{1,0:T(2,128)} %bitcast.3, s32[4]{0:T(128)} %block_ref.1, bf16[8,7168]{1,0:T(8,128)(2,1)} %x_ref.1, bf16[7168,256]{1,0:T(8,128)(2,1)} %wg_ref.1, bf16[7168,256]{1,0:T(8,128)(2,1)} %wu_ref.1, bf16[256,7168]{1,0:T(8,128)(2,1)} %wd_ref.1), custom_call_target="tpu_custom_call" | custom-call | tf_op jit(solution)/shard_map/pallas_call | solution.py:236
  37.8 1.6 %convert_element_type.3 = bf16[8,7168]{1,0:T(8,128)(2,1)} convert(f32[8,7168]{1,0:T(8,128)} %shard_map.73) | non-fusion elementwise | flops 57344 | bytes 344064 | tf_op jit(solution)/shard_map/convert_element_type | solution.py:267
